TPU v7x, 32 devices: a whole 2x2x4 slice. The times are simulated.
32 devices in a mesh: groups: 2 (over x), dom: 16 (over z, y, core).
Axes of the slice: x: 2, y: 2, z: 4, core: 2. Of those that a mesh axis runs over, the one named last changes fastest.
Arguments:
- grid_in: bfloat16 [32768, 384], P(('groups', 'dom')), parts along dimension 0, may hold values from -6 to 6
- mesh_static: bfloat16 [8192, 512], P('dom'), may hold values from -6 to 6
- block_links: int32 [128, 4], replicated, may hold values from 0 to 127, as said below
- grid_links: int32 [256], P('dom'), may hold values from 0 to 7, as said below
- w_encode: bfloat16 [384, 512], replicated, may hold values from -0.3125 to 0.3125
- w_send: bfloat16 [2, 512, 512], replicated, may hold values from -0.25 to 0.25
- w_recv: bfloat16 [2, 512, 512], replicated, may hold values from -0.25 to 0.25
- edge_bias: float32 [2, 512], replicated, may hold values from -4 to 4
- w_self: bfloat16 [2, 512, 512], replicated, may hold values from -0.25 to 0.25
- w_gathered: bfloat16 [2, 512, 512], replicated, may hold values from -0.25 to 0.25
- node_bias: float32 [2, 512], replicated, may hold values from -4 to 4
- w_out: bfloat16 [2, 512, 512], replicated, may hold values from -0.25 to 0.25
- norm_gain: float32 [2, 512], replicated, may hold values from 0.5 to 2
- w_decode: bfloat16 [512, 512], replicated, may hold values from -0.25 to 0.25
- w_final: bfloat16 [512, 256], replicated, may hold values from -0.25 to 0.25
Outputs:
- prediction: float32 [32768, 256], P(('groups', 'dom')), parts along dimension 0
There are 2 independent parts, one for each index of `groups`. A program takes and returns all parts, laid end to end along the dimension named above; an argument that names none is the same for every part. Nothing has to cross between parts.
Inputs may be any that keep to these rules, and one draw needn't show every extreme that they name: `block_links`: every named block is a block of the same partition (ids p * 8 to p * 8 + 7) or one of the first 3 blocks of the partition whose index differs by 1 or 2, counted cyclically over the partitions; a partition names at most 2 distinct blocks of each such neighbour, and exactly 2 for some pair. `grid_links`: every mesh block of a partition is tied to one or more grid blocks of that partition.
All inputs are finite; a program needn't handle non-finite values.
Results may differ from a plain program's by a relative error of at most 0.009.
Values may be sent and summed in bfloat16 or wider, within the bound.
A program may use at most 64 MiB of HBM per device.

v0:
```python
import jax
import jax.numpy as jnp
from jax import lax
from jax.sharding import PartitionSpec as P

BLOCK = 64
K = 4
NBD = 3
LAYERS = 2


def shifted(block, axis, distance):
    devices = range(lax.axis_size(axis))
    route = [((i - distance) % len(devices), i) for i in devices]
    return lax.ppermute(block, axis, route)


def fetch(state, links_mine, device, ndevices, blocks):
    width = state.shape[1]
    tiles = state.reshape(blocks, BLOCK, width)
    owner = links_mine // blocks
    within = links_mine % blocks
    border = tiles[:NBD]
    shifts = (1, -1, 2, -2)
    arrived = [shifted(border, "dom", offset) for offset in shifts]
    where_row = within
    for number, offset in enumerate(shifts):
        source = (device - offset) % ndevices
        where_row = jnp.where(owner == source, blocks + number * NBD + within, where_row)
    return (jnp.concatenate(arrived, axis=0), where_row)


def local(
    grid_in,
    mesh_static,
    block_links,
    grid_links,
    w_encode,
    w_send,
    w_recv,
    edge_bias,
    w_self,
    w_gathered,
    node_bias,
    w_out,
    norm_gain,
    w_decode,
    w_final,
):
    f32 = jnp.float32
    device = lax.axis_index("dom")
    ndevices = lax.axis_size("dom")
    width = mesh_static.shape[1]
    blocks = mesh_static.shape[0] // BLOCK
    grid_blocks = grid_in.shape[0] // BLOCK
    encoded = jax.nn.silu(jnp.dot(grid_in, w_encode, preferred_element_type=f32)).astype(
        jnp.bfloat16
    )
    spreader = (grid_links[None, :] == jnp.arange(blocks, dtype=jnp.int32)[:, None]).astype(
        jnp.bfloat16
    )
    mesh_sum = jnp.dot(
        spreader, encoded.reshape(grid_blocks, BLOCK * width), preferred_element_type=f32
    ).reshape(-1, width)
    state = (mesh_static.astype(f32) + mesh_sum).astype(jnp.bfloat16)
    links_mine = lax.dynamic_slice_in_dim(block_links, device * blocks, blocks, 0)
    for layer in range(LAYERS):
        source = jnp.dot(state, w_send[layer], preferred_element_type=f32).reshape(
            blocks, 1, BLOCK, width
        )
        remote_tiles, where_row = fetch(state, links_mine, device, ndevices, blocks)
        own_proj = jnp.dot(state, w_recv[layer], preferred_element_type=f32)
        remote_proj = jnp.dot(
            remote_tiles.reshape(-1, width), w_recv[layer], preferred_element_type=f32
        )
        table = jnp.concatenate([own_proj, remote_proj], axis=0).reshape(-1, BLOCK, width)
        projected_in = jnp.take(table, where_row.reshape(-1), axis=0).reshape(
            blocks, K, BLOCK, width
        )
        edges = jax.nn.silu(source + projected_in + edge_bias[layer])
        gathered = jnp.sum(edges, axis=1).reshape(-1, width).astype(jnp.bfloat16)
        update = jax.nn.silu(
            jnp.dot(state, w_self[layer], preferred_element_type=f32)
            + jnp.dot(gathered, w_gathered[layer], preferred_element_type=f32)
            + node_bias[layer]
        ).astype(jnp.bfloat16)
        projected = jnp.dot(update, w_out[layer], preferred_element_type=f32)
        center = jnp.mean(projected, axis=-1, keepdims=True)
        spread = jnp.mean((projected - center) ** 2, axis=-1, keepdims=True)
        normed = (projected - center) / jnp.sqrt(spread + 1e-05) * norm_gain[layer]
        state = (state.astype(f32) + normed).astype(jnp.bfloat16)
    tied = jnp.take(state.reshape(blocks, BLOCK, width), grid_links, axis=0).reshape(-1, width)
    decoded = jax.nn.silu(
        jnp.dot(tied, w_decode, preferred_element_type=f32) + encoded.astype(f32)
    ).astype(jnp.bfloat16)
    return jnp.dot(decoded, w_final, preferred_element_type=f32)


def solution(mesh):
    in_specs = (
        P(("groups", "dom"), None),
        P("dom", None),
        P(),
        P("dom"),
        P(),
        P(),
        P(),
        P(),
        P(),
        P(),
        P(),
        P(),
        P(),
        P(),
        P(),
    )
    out_specs = P(("groups", "dom"), None)
    return jax.shard_map(local, mesh=mesh, in_specs=in_specs, out_specs=out_specs, check_vma=False)
```

profile of v0, /device:TPU:0, one launch (start us, length us, event | category | flops | bytes accessed | tf_op | source)
XLA Modules:
  0.0 71.2 jit_solution(1514184609653487224)
XLA Ops:
  0.0 1.1 %copy-done = bf16[1024,384]{1,0:T(8,128)(2,1)S(1)} copy-done((bf16[1024,384]{1,0:T(8,128)(2,1)S(1)}, bf16[1024,384]{1,0:T(8,128)(2,1)}, u32[]{:S(2)}) %copy-start) | copy-done | bytes 786456
  1.1 2.0 %multiply_convert_fusion.1 = bf16[1024,512]{1,0:T(8,128)(2,1)S(1)} fusion(bf16[1024,384]{1,0:T(8,128)(2,1)S(1)} %copy-done, bf16[384,512]{1,0:T(8,128)(2,1)} %param.21), kind=kOutput, calls=%fused_computation.10 | convolution fusion | flops 405274624 | bytes 2228224 | tf_op jit(solution)/shard_map/dot_general | solution.py:56
  3.1 1.0 %copy-done.7 = bf16[1024,512]{1,0:T(8,128)(2,1)} copy-done((bf16[1024,512]{1,0:T(8,128)(2,1)}, bf16[1024,512]{1,0:T(8,128)(2,1)S(1)}, u32[]{:S(2)}) %copy-start.7) | copy-done | bytes 1048600
  4.1 0.5 reshape.107
  4.6 0.3 fusion.46
  5.4 0.7 slice.88
  6.1 0.5 collective-permute-start
  6.5 5.0 %collective-permute-start.1 = (bf16[3,64,512]{2,1,0:T(8,128)(2,1)}, bf16[3,64,512]{2,1,0:T(8,128)(2,1)}, u32[]{:S(2)}, u32[]{:S(2)}) collective-permute-start(bf16[3,64,512]{2,1,0:T(8,128)(2,1)} %bitcast.5), channel_id=1, source_target_pairs={{1,0},{2,1},{3,2},{4,3},{5,4},{6,5},{7,6},{8,7},{9,8},{10,9},{11,1... | collective-permute-start | bytes 589832 | tf_op jit(solution)/shard_map/ppermute | solution.py:15
  11.5 4.7 %collective-permute-start.3 = (bf16[3,64,512]{2,1,0:T(8,128)(2,1)}, bf16[3,64,512]{2,1,0:T(8,128)(2,1)}, u32[]{:S(2)}, u32[]{:S(2)}) collective-permute-start(bf16[3,64,512]{2,1,0:T(8,128)(2,1)} %bitcast.5), channel_id=1, source_target_pairs={{2,0},{3,1},{4,2},{5,3},{6,4},{7,5},{8,6},{9,7},{10,8},{11,9},{12,... | collective-permute-start | bytes 589832 | tf_op jit(solution)/shard_map/ppermute | solution.py:15
  16.6 2.5 %fusion.22 = f32[512,512]{1,0:T(8,128)} fusion(bf16[512,512]{1,0:T(8,128)(2,1)S(1)} %add_convert_fusion.2, bf16[2,512,512]{2,1,0:T(8,128)(2,1)} %param.23), kind=kOutput, calls=%fused_computation.43 | convolution fusion | flops 268435456 | bytes 2097152 | tf_op jit(solution)/shard_map/dot_general | solution.py:72
  19.0 2.5 %fusion.26 = f32[512,512]{1,0:T(8,128)} fusion(bf16[512,512]{1,0:T(8,128)(2,1)S(1)} %add_convert_fusion.2, bf16[2,512,512]{2,1,0:T(8,128)(2,1)} %param.25), kind=kOutput, calls=%fused_computation.47 | convolution fusion | flops 268435456 | bytes 2097152 | tf_op jit(solution)/shard_map/dot_general | solution.py:83
  21.7 1.5 %fusion.24 = f32[8,64,512]{2,1,0:T(8,128)} fusion(bf16[8,64,512]{2,1,0:T(8,128)(2,1)S(1)} %bitcast.88, bf16[2,512,512]{2,1,0:T(8,128)(2,1)S(1)} %copy-done.10), kind=kOutput, calls=%fused_computation.45 | convolution fusion | flops 268435456 | bytes 2097152 | tf_op jit(solution)/shard_map/dot_general | solution.py:68
  23.2 2.1 %collective-permute-done.3 = bf16[3,64,512]{2,1,0:T(8,128)(2,1)} collective-permute-done((bf16[3,64,512]{2,1,0:T(8,128)(2,1)}, bf16[3,64,512]{2,1,0:T(8,128)(2,1)}, u32[]{:S(2)}, u32[]{:S(2)}) %collective-permute-start.3) | collective-permute-done | bytes 196640 | tf_op jit(solution)/shard_map/ppermute | solution.py:15
  25.3 1.3 %pad_maximum_fusion.2 = bf16[12,64,512]{2,1,0:T(8,128)(2,1)S(1)} fusion(bf16[3,64,512]{2,1,0:T(8,128)(2,1)} %collective-permute-done.3, bf16[3,64,512]{2,1,0:T(8,128)(2,1)} %collective-permute-done.2, bf16[3,64,512]{2,1,0:T(8,128)(2,1)} %collective-permute-done.1, bf16[3,64,512]{2,1,0:T(8,128)(2,1)} %collective-permute-done), kind=kLoop, calls=%fused_computation.27 | loop fusion | flops 1179648 | bytes 1572864 | tf_op jit(solution)/shard_map/concatenate | solution.py:30
  26.6 0.6 fusion.20
  27.2 1.5 %pad_maximum_fusion = f32[1280,512]{1,0:T(8,128)S(1)} fusion(f32[768,512]{1,0:T(8,128)S(1)} %fusion.20, f32[512,512]{1,0:T(8,128)} %fusion.22), kind=kLoop, calls=%fused_computation.5 | loop fusion | flops 655360 | bytes 5242880 | tf_op jit(solution)/shard_map/concatenate | solution.py:76
  28.7 2.8 %gather_fusion.1 = f32[32,64,512]{2,1,0:T(8,128)} fusion(f32[20,64,512]{2,1,0:T(8,128)S(1)} %bitcast.86, s32[1024]{0:T(1024)S(1)} %pad_clamp_fusion.1), kind=kCustom, calls=%fused_computation.clone | custom fusion | bytes 8388736 | tf_op jit(solution)/shard_map/jit(_take)/gather | solution.py:77
  31.4 4.9 %multiply_reduce_fusion.1 = bf16[8,64,512]{2,1,0:T(8,128)(2,1)} fusion(f32[512]{0:T(512)S(1)} %bitcast.101, f32[8,64,512]{2,1,0:T(8,128)} %fusion.24, f32[32,64,512]{2,1,0:T(8,128)} %gather_fusion.1, pred[32]{0:T(512)(128)(4,1)S(1)} %compare_and_fusion), kind=kLoop, calls=%fused_computation.4 | loop fusion | flops 8126464 | bytes 5769248 | tf_op jit(solution)/shard_map/reduce_sum | solution.py:81
  36.3 2.7 %fusion.58 = (f32[512]{0:T(512)S(1)}, f32[512,512]{1,0:T(8,128)S(1)}) fusion(bf16[2,512,512]{2,1,0:T(8,128)(2,1)} %param.28, f32[512,512]{1,0:T(8,128)} %fusion.26, bf16[512,512]{1,0:T(8,128)(2,1)} %bitcast.93, f32[512]{0:T(512)S(1)} %bitcast.103, bf16[2,512,512]{2,1,0:T(8,128)(2,1)} %param.26), kind=kOutput, calls=%fused_computation.95 | convolution fusion | flops 538967552 | bytes 3674112 | tf_op jit(solution)/shard_map/dot_general | solution.py:87
  39.7 4.4 %collective-permute-start.5 = (bf16[3,64,512]{2,1,0:T(8,128)(2,1)S(1)}, bf16[3,64,512]{2,1,0:T(8,128)(2,1)S(1)}, u32[]{:S(2)}, u32[]{:S(2)}) collective-permute-start(bf16[3,64,512]{2,1,0:T(8,128)(2,1)S(1)} %bitcast.95), channel_id=1, source_target_pairs={{1,0},{2,1},{3,2},{4,3},{5,4},{6,5},{7,6},{8,7},{9,8},{10,9},{11,1... | collective-permute-start | bytes 589832 | tf_op jit(solution)/shard_map/ppermute | solution.py:15
  44.2 4.7 %collective-permute-start.7 = (bf16[3,64,512]{2,1,0:T(8,128)(2,1)S(1)}, bf16[3,64,512]{2,1,0:T(8,128)(2,1)S(1)}, u32[]{:S(2)}, u32[]{:S(2)}) collective-permute-start(bf16[3,64,512]{2,1,0:T(8,128)(2,1)S(1)} %bitcast.97), channel_id=1, source_target_pairs={{2,0},{3,1},{4,2},{5,3},{6,4},{7,5},{8,6},{9,7},{10,8},{11,9},{12,... | collective-permute-start | bytes 589832 | tf_op jit(solution)/shard_map/ppermute | solution.py:15
  48.9 0.4 fusion.11
  49.3 1.4 %fusion.15 = f32[512,512]{1,0:T(8,128)} fusion(bf16[512,512]{1,0:T(8,128)(2,1)S(1)} %add_convert_fusion.1, bf16[2,512,512]{2,1,0:T(8,128)(2,1)S(1)} %copy-done.9), kind=kOutput, calls=%fused_computation.37 | convolution fusion | flops 268435456 | bytes 2097152 | tf_op jit(solution)/shard_map/dot_general | solution.py:83
  50.8 1.4 %fusion.13 = f32[8,64,512]{2,1,0:T(8,128)} fusion(bf16[8,64,512]{2,1,0:T(8,128)(2,1)S(1)} %bitcast.87, bf16[2,512,512]{2,1,0:T(8,128)(2,1)S(1)} %copy-done.11), kind=kOutput, calls=%fused_computation.35 | convolution fusion | flops 268435456 | bytes 2097152 | tf_op jit(solution)/shard_map/dot_general | solution.py:68
  52.2 0.4 collective-permute-done.6
  52.6 2.7 %collective-permute-done.7 = bf16[3,64,512]{2,1,0:T(8,128)(2,1)S(1)} collective-permute-done((bf16[3,64,512]{2,1,0:T(8,128)(2,1)S(1)}, bf16[3,64,512]{2,1,0:T(8,128)(2,1)S(1)}, u32[]{:S(2)}, u32[]{:S(2)}) %collective-permute-start.7) | collective-permute-done | bytes 196640 | tf_op jit(solution)/shard_map/ppermute | solution.py:15
  55.5 0.6 fusion.9
  56.3 2.8 %gather_fusion.2 = f32[32,64,512]{2,1,0:T(8,128)} fusion(f32[20,64,512]{2,1,0:T(8,128)S(1)} %bitcast.85, s32[1024]{0:T(1024)S(1)} %pad_clamp_fusion.1), kind=kCustom, calls=%fused_computation.1.clone | custom fusion | bytes 8388736 | tf_op jit(solution)/shard_map/jit(_take)/gather | solution.py:77
  59.0 4.9 %multiply_reduce_fusion = bf16[8,64,512]{2,1,0:T(8,128)(2,1)} fusion(f32[512]{0:T(512)S(1)} %bitcast.99, f32[8,64,512]{2,1,0:T(8,128)} %fusion.13, f32[32,64,512]{2,1,0:T(8,128)} %gather_fusion.2, pred[32]{0:T(512)(128)(4,1)S(1)} %compare_and_fusion), kind=kLoop, calls=%fused_computation.3 | loop fusion | flops 8126464 | bytes 5769248 | tf_op jit(solution)/shard_map/reduce_sum | solution.py:81
  64.0 2.4 %fusion.61 = (f32[512]{0:T(512)S(1)}, f32[512,512]{1,0:T(8,128)S(1)}) fusion(bf16[2,512,512]{2,1,0:T(8,128)(2,1)} %param.28, f32[512,512]{1,0:T(8,128)S(1)} %copy-done.8, bf16[512,512]{1,0:T(8,128)(2,1)} %bitcast.92, f32[512]{0:T(512)S(1)} %bitcast.102, bf16[2,512,512]{2,1,0:T(8,128)(2,1)} %param.26), kind=kOutput, calls=%fused_computation.96 | convolution fusion | flops 538967552 | bytes 3674112 | tf_op jit(solution)/shard_map/dot_general | solution.py:87
  66.9 0.6 gather_fusion
  67.8 3.4 %fusion.2 = f32[1024,256]{1,0:T(8,128)} fusion(bf16[512,256]{1,0:T(8,128)(2,1)} %param.31, bf16[1024,512]{1,0:T(8,128)(2,1)} %copy-done.7, bf16[1024,512]{1,0:T(8,128)(2,1)S(1)} %bitcast_select_fusion, bf16[512,512]{1,0:T(8,128)(2,1)S(1)} %copy-done.18), kind=kOutput, calls=%fused_computation.15 | convolution fusion | flops 808976384 | bytes 3932160 | tf_op jit(solution)/shard_map/dot_general | solution.py:96
  (72 shorter events, 2.6 us)
Async XLA Ops:
  0.0 1.1 %copy-start = (bf16[1024,384]{1,0:T(8,128)(2,1)S(1)}, bf16[1024,384]{1,0:T(8,128)(2,1)}, u32[]{:S(2)}) copy-start(bf16[1024,384]{1,0:T(8,128)(2,1)} %param.17) | copy-start | bytes 2359300
  0.0 4.6 %copy-start.17 = (s32[16]{0:T(128)S(1)}, s32[16]{0:T(128)}, u32[]{:S(2)}) copy-start(s32[16]{0:T(128)} %param.20) | copy-start | bytes 196
  3.1 1.0 %copy-start.7 = (bf16[1024,512]{1,0:T(8,128)(2,1)}, bf16[1024,512]{1,0:T(8,128)(2,1)S(1)}, u32[]{:S(2)}) copy-start(bf16[1024,512]{1,0:T(8,128)(2,1)S(1)} %multiply_convert_fusion.1) | copy-start | bytes 3145732
  4.1 1.1 %copy-start.12 = (bf16[512,512]{1,0:T(8,128)(2,1)S(1)}, bf16[512,512]{1,0:T(8,128)(2,1)}, u32[]{:S(2)}) copy-start(bf16[512,512]{1,0:T(8,128)(2,1)} %param.18) | copy-start | bytes 1572868
  4.1 12.2 %copy-start.16 = (s32[128,4]{0,1:T(4,128)S(1)}, s32[128,4]{0,1:T(4,128)}, u32[]{:S(2)}) copy-start(s32[128,4]{0,1:T(4,128)} %param.19) | copy-start | bytes 6148
  4.6 14.4 %copy-start.13 = (f32[2,512]{1,0:T(2,128)S(1)}, f32[2,512]{1,0:T(2,128)}, u32[]{:S(2)}) copy-start(f32[2,512]{1,0:T(2,128)} %param.24) | copy-start | bytes 12292
  4.9 16.6 %copy-start.14 = (f32[2,512]{1,0:T(2,128)S(1)}, f32[2,512]{1,0:T(2,128)}, u32[]{:S(2)}) copy-start(f32[2,512]{1,0:T(2,128)} %param.27) | copy-start | bytes 12292
  4.9 16.6 %copy-start.15 = (f32[2,512]{1,0:T(2,128)S(1)}, f32[2,512]{1,0:T(2,128)}, u32[]{:S(2)}) copy-start(f32[2,512]{1,0:T(2,128)} %param.29) | copy-start | bytes 12292
  5.3 21.3 %copy-start.3 = (bf16[512,512]{1,0:T(8,128)(2,1)}, bf16[512,512]{1,0:T(8,128)(2,1)S(1)}, u32[]{:S(2)}) copy-start(bf16[512,512]{1,0:T(8,128)(2,1)S(1)} %add_convert_fusion.2) | copy-start | bytes 1572868
  5.3 16.4 %copy-start.10 = (bf16[2,512,512]{2,1,0:T(8,128)(2,1)S(1)}, bf16[2,512,512]{2,1,0:T(8,128)(2,1)}, u32[]{:S(2)}) copy-start(bf16[2,512,512]{2,1,0:T(8,128)(2,1)} %param.22) | copy-start | bytes 3145732
  5.4 21.3 %copy-start.5 = (bf16[2,512,512]{2,1,0:T(8,128)(2,1)S(1)}, bf16[2,512,512]{2,1,0:T(8,128)(2,1)}, u32[]{:S(2)}) copy-start(bf16[2,512,512]{2,1,0:T(8,128)(2,1)} %param.23) | copy-start | bytes 3145732
  6.1 17.1 %collective-permute-start = (bf16[3,64,512]{2,1,0:T(8,128)(2,1)}, bf16[3,64,512]{2,1,0:T(8,128)(2,1)}, u32[]{:S(2)}, u32[]{:S(2)}) collective-permute-start(bf16[3,64,512]{2,1,0:T(8,128)(2,1)} %bitcast.5), channel_id=1, source_target_pairs={{15,0},{0,1},{1,2},{2,3},{3,4},{4,5},{5,6},{6,7},{7,8},{8,9},{9,10... | collective-permute-start | bytes 589832 | tf_op jit(solution)/shard_map/ppermute | solution.py:15
  6.5 16.7 %collective-permute-start.1 = (bf16[3,64,512]{2,1,0:T(8,128)(2,1)}, bf16[3,64,512]{2,1,0:T(8,128)(2,1)}, u32[]{:S(2)}, u32[]{:S(2)}) collective-permute-start(bf16[3,64,512]{2,1,0:T(8,128)(2,1)} %bitcast.5), channel_id=1, source_target_pairs={{1,0},{2,1},{3,2},{4,3},{5,4},{6,5},{7,6},{8,7},{9,8},{10,9},{11,1... | collective-permute-start | bytes 589832 | tf_op jit(solution)/shard_map/ppermute | solution.py:15
  11.5 11.7 %collective-permute-start.2 = (bf16[3,64,512]{2,1,0:T(8,128)(2,1)}, bf16[3,64,512]{2,1,0:T(8,128)(2,1)}, u32[]{:S(2)}, u32[]{:S(2)}) collective-permute-start(bf16[3,64,512]{2,1,0:T(8,128)(2,1)} %bitcast.5), channel_id=1, source_target_pairs={{14,0},{15,1},{0,2},{1,3},{2,4},{3,5},{4,6},{5,7},{6,8},{7,9},{8,1... | collective-permute-start | bytes 589832 | tf_op jit(solution)/shard_map/ppermute | solution.py:15
  11.5 13.8 %collective-permute-start.3 = (bf16[3,64,512]{2,1,0:T(8,128)(2,1)}, bf16[3,64,512]{2,1,0:T(8,128)(2,1)}, u32[]{:S(2)}, u32[]{:S(2)}) collective-permute-start(bf16[3,64,512]{2,1,0:T(8,128)(2,1)} %bitcast.5), channel_id=1, source_target_pairs={{2,0},{3,1},{4,2},{5,3},{6,4},{7,5},{8,6},{9,7},{10,8},{11,9},{12,... | collective-permute-start | bytes 589832 | tf_op jit(solution)/shard_map/ppermute | solution.py:15
  36.3 3.0 %copy-start.4 = (bf16[512,512]{1,0:T(8,128)(2,1)S(1)}, bf16[512,512]{1,0:T(8,128)(2,1)}, u32[]{:S(2)}) copy-start(bf16[512,512]{1,0:T(8,128)(2,1)} %copy-done.3) | copy-start | bytes 1572868
  36.3 12.6 %copy-start.6 = (bf16[2,512,512]{2,1,0:T(8,128)(2,1)S(1)}, bf16[2,512,512]{2,1,0:T(8,128)(2,1)}, u32[]{:S(2)}) copy-start(bf16[2,512,512]{2,1,0:T(8,128)(2,1)} %param.23) | copy-start | bytes 3145732
  39.0 10.3 %copy-start.9 = (bf16[2,512,512]{2,1,0:T(8,128)(2,1)S(1)}, bf16[2,512,512]{2,1,0:T(8,128)(2,1)}, u32[]{:S(2)}) copy-start(bf16[2,512,512]{2,1,0:T(8,128)(2,1)} %param.25) | copy-start | bytes 3145732
  39.1 11.7 %copy-start.11 = (bf16[2,512,512]{2,1,0:T(8,128)(2,1)S(1)}, bf16[2,512,512]{2,1,0:T(8,128)(2,1)}, u32[]{:S(2)}) copy-start(bf16[2,512,512]{2,1,0:T(8,128)(2,1)} %param.22) | copy-start | bytes 3145732
  39.6 11.1 %copy-start.1 = (bf16[512,512]{1,0:T(8,128)(2,1)}, bf16[512,512]{1,0:T(8,128)(2,1)S(1)}, u32[]{:S(2)}) copy-start(bf16[512,512]{1,0:T(8,128)(2,1)S(1)} %add_convert_fusion.1) | copy-start | bytes 1572868
  39.7 12.5 %collective-permute-start.4 = (bf16[3,64,512]{2,1,0:T(8,128)(2,1)S(1)}, bf16[3,64,512]{2,1,0:T(8,128)(2,1)S(1)}, u32[]{:S(2)}, u32[]{:S(2)}) collective-permute-start(bf16[3,64,512]{2,1,0:T(8,128)(2,1)S(1)} %bitcast.94), channel_id=1, source_target_pairs={{15,0},{0,1},{1,2},{2,3},{3,4},{4,5},{5,6},{6,7},{7,8},{8,9},{9,10... | collective-permute-start | bytes 589832 | tf_op jit(solution)/shard_map/ppermute | solution.py:15
  39.7 12.5 %collective-permute-start.5 = (bf16[3,64,512]{2,1,0:T(8,128)(2,1)S(1)}, bf16[3,64,512]{2,1,0:T(8,128)(2,1)S(1)}, u32[]{:S(2)}, u32[]{:S(2)}) collective-permute-start(bf16[3,64,512]{2,1,0:T(8,128)(2,1)S(1)} %bitcast.95), channel_id=1, source_target_pairs={{1,0},{2,1},{3,2},{4,3},{5,4},{6,5},{7,6},{8,7},{9,8},{10,9},{11,1... | collective-permute-start | bytes 589832 | tf_op jit(solution)/shard_map/ppermute | solution.py:15
  44.2 8.5 %collective-permute-start.6 = (bf16[3,64,512]{2,1,0:T(8,128)(2,1)S(1)}, bf16[3,64,512]{2,1,0:T(8,128)(2,1)S(1)}, u32[]{:S(2)}, u32[]{:S(2)}) collective-permute-start(bf16[3,64,512]{2,1,0:T(8,128)(2,1)S(1)} %bitcast.96), channel_id=1, source_target_pairs={{14,0},{15,1},{0,2},{1,3},{2,4},{3,5},{4,6},{5,7},{6,8},{7,9},{8,1... | collective-permute-start | bytes 589832 | tf_op jit(solution)/shard_map/ppermute | solution.py:15
  44.2 11.2 %collective-permute-start.7 = (bf16[3,64,512]{2,1,0:T(8,128)(2,1)S(1)}, bf16[3,64,512]{2,1,0:T(8,128)(2,1)S(1)}, u32[]{:S(2)}, u32[]{:S(2)}) collective-permute-start(bf16[3,64,512]{2,1,0:T(8,128)(2,1)S(1)} %bitcast.97), channel_id=1, source_target_pairs={{2,0},{3,1},{4,2},{5,3},{6,4},{7,5},{8,6},{9,7},{10,8},{11,9},{12,... | collective-permute-start | bytes 589832 | tf_op jit(solution)/shard_map/ppermute | solution.py:15
  59.0 4.9 %copy-start.8 = (f32[512,512]{1,0:T(8,128)S(1)}, f32[512,512]{1,0:T(8,128)}, u32[]{:S(2)}) copy-start(f32[512,512]{1,0:T(8,128)} %fusion.15) | copy-start | bytes 3145732
  64.0 2.7 %copy-start.2 = (bf16[512,512]{1,0:T(8,128)(2,1)S(1)}, bf16[512,512]{1,0:T(8,128)(2,1)}, u32[]{:S(2)}) copy-start(bf16[512,512]{1,0:T(8,128)(2,1)} %copy-done.1) | copy-start | bytes 1572868
  66.4 1.4 %copy-start.18 = (bf16[512,512]{1,0:T(8,128)(2,1)S(1)}, bf16[512,512]{1,0:T(8,128)(2,1)}, u32[]{:S(2)}) copy-start(bf16[512,512]{1,0:T(8,128)(2,1)} %param.30) | copy-start | bytes 1572868
where the time goes:
time: 71.6 us; the launch traced here: 71.2 us
  matrix products  21.5 us (30%)
  starting transfers between devices  19.4 us (27%)
  other arithmetic  14.5 us (20%)
  local copies, waits for them, and re-layouts  10.1 us (14%)
  waiting for transfers between devices  5.24 us (7%)
    ppermute x8, starting transfers between devices, shifted(): return lax.ppermute(block, axis, route)  19.4 us
    reduce_sum x2, other arithmetic, local(): gathered = jnp.sum(edges, axis=1).reshape(-1, width).astype(jnp.bfloat16)  9.81 us
    gather x2, local copies, waits for them, and re-layouts, local(): jnp.take(table, where_row.reshape(-1), axis=0)  5.53 us
    ppermute x8, waiting for transfers between devices, shifted(): return lax.ppermute(block, axis, route)  5.24 us
    dot_general x2, matrix products, local(): projected = jnp.dot(update, w_out[layer], preferred_element_type=f32)  5.11 us
    dot_general x2, matrix products, local(): jnp.dot(state, w_self[layer], preferred_element_type=f32)  3.86 us
    dot_general x1, matrix products, local(): return jnp.dot(decoded, w_final, preferred_element_type=f32)  3.37 us
    dot_general x2, matrix products, local(): jnp.dot(state, w_send[layer], preferred_element_type=f32)  2.9 us
  transfers between devices with their start and end apart: 8, of which 3 were waited for; matrix products, arithmetic and copies ran while one was open for 14% of the time, Pallas kernels for 0%

commit v1 on v0

v1 whole, which is shorter than its diff:
```python
import functools

import jax
import jax.numpy as jnp
from jax import lax
from jax.experimental import pallas as pl
from jax.experimental.pallas import tpu as pltpu
from jax.sharding import PartitionSpec as P

BLOCK = 64
K = 4
NBD = 3
CAP = 2
LAYERS = 2
OFFSETS = (1, -1, 2, -2)
HALF = 4
CHUNK = 16
MESH_ID = pl.DeviceIdType.MESH


def dot(a, b):
    return jnp.dot(a, b, preferred_element_type=jnp.float32)


def silu_of_half(h):
    return h + h * jnp.tanh(h)


def span(values, owner, blocks):
    low, high = NBD - 1, 0
    for value in values:
        within = value - owner * blocks
        named = (within >= 0) & (within < blocks)
        low = jnp.where(named, jnp.minimum(low, within), low)
        high = jnp.where(named, jnp.maximum(high, within), high)
    return low, high


def kernel(
    n,
    blocks,
    grid_blocks,
    grid_links,
    links,
    grid_hbm,
    static_hbm,
    *refs,
):
    weights_hbm = refs[:11]
    out_hbm = refs[11]
    (
        grid_in,
        static,
        w_encode,
        w_send,
        w_recv,
        edge_bias,
        w_self,
        w_gathered,
        node_bias,
        w_out,
        norm_gain,
        w_decode,
        w_final,
        encoded,
        state,
        source,
        own,
        table,
        gathered,
        stage,
        arrived,
        out,
        where_row,
        w_sem,
        layer_sem,
        grid_sem,
        out_sem,
        send_sem,
        recv_sem,
    ) = refs[12:]
    me = lax.axis_index("dom")
    sides = [lax.rem(me + offset + n, n) for offset in OFFSETS]
    rows = blocks * BLOCK
    grid_rows = grid_blocks * BLOCK
    half = HALF * BLOCK
    width = state.shape[3]

    barrier = pltpu.get_barrier_semaphore()
    for side in sides:
        pl.semaphore_signal(barrier, inc=1, device_id={"dom": side}, device_id_type=MESH_ID)

    copies = {}

    def fetch(name, src, dst, sem):
        copies[name] = pltpu.make_async_copy(src, dst, sem)
        copies[name].start()

    (
        w_encode_h,
        w_send_h,
        w_recv_h,
        edge_bias_h,
        w_self_h,
        w_gathered_h,
        node_bias_h,
        w_out_h,
        norm_gain_h,
        w_decode_h,
        w_final_h,
    ) = weights_hbm
    fetch("w_encode", w_encode_h, w_encode, w_sem.at[0])
    for first in range(0, grid_rows, half):
        piece = pl.ds(first, half)
        fetch(("grid", first), grid_hbm.at[piece], grid_in.at[piece], grid_sem.at[first // half])
    fetch("static", static_hbm, static, w_sem.at[1])
    fetch("edge_bias", edge_bias_h, edge_bias, w_sem.at[2])
    fetch("node_bias", node_bias_h, node_bias, w_sem.at[3])
    fetch("norm_gain", norm_gain_h, norm_gain, w_sem.at[4])
    for layer in range(LAYERS):
        for number, (src, dst) in enumerate(
            (
                (w_send_h, w_send),
                (w_recv_h, w_recv),
                (w_self_h, w_self),
                (w_gathered_h, w_gathered),
                (w_out_h, w_out),
            )
        ):
            fetch(("layer", layer, number), src.at[layer], dst.at[layer], layer_sem.at[layer, number])
    fetch("w_decode", w_decode_h, w_decode, w_sem.at[5])
    fetch("w_final", w_final_h, w_final, w_sem.at[6])

    def rows_of(owner):
        return [links[k, owner * blocks + b] for b in range(blocks) for k in range(K)]

    wanted = [span(rows_of(side), me, blocks) for side in sides]
    named = [span(rows_of(me), side, blocks) for side in sides]
    for b in range(blocks):
        for k in range(K):
            value = links[k, me * blocks + b]
            row = jnp.clip(value - me * blocks, 0, blocks - 1)
            for number, side in enumerate(sides):
                within = value - side * blocks
                theirs = (within >= 0) & (within < blocks)
                slot = jnp.where(within == named[number][0], 0, 1)
                row = jnp.where(theirs, blocks + number * CAP + slot, row)
            where_row[b * K + k] = row

    copies["w_encode"].wait()
    for first in range(0, grid_rows, half):
        copies["grid", first].wait()
        piece = pl.ds(first, half)
        encoded[piece] = silu_of_half(0.5 * dot(grid_in[piece], w_encode[...])).astype(jnp.bfloat16)

    column = lax.broadcasted_iota(jnp.int32, (8, grid_rows), 1)
    key = jnp.zeros((8, grid_rows), jnp.int32)
    for g in range(grid_blocks):
        key = jnp.where(column // BLOCK == g, grid_links[g] * BLOCK - g * BLOCK, key)
    key = (key + column)[:1]
    copies["static"].wait()

    sends = {}

    def ship(layer):
        for number, side in enumerate(sides):
            for slot in range(CAP):
                stage[layer, number, slot] = state[layer, wanted[number][slot]]
            sends[layer, number] = pltpu.make_async_remote_copy(
                src_ref=stage.at[layer, number],
                dst_ref=arrived.at[layer, number ^ 1],
                send_sem=send_sem.at[layer, number],
                recv_sem=recv_sem.at[layer, number ^ 1],
                device_id={"dom": side},
                device_id_type=MESH_ID,
            )
            sends[layer, number].start()

    for first in range(0, rows, half):
        piece = pl.ds(first, half)
        line = lax.broadcasted_iota(jnp.int32, (half, grid_rows), 0) + first
        spreader = jnp.where(line == key, 1.0, 0.0).astype(jnp.bfloat16)
        mesh_sum = dot(spreader, encoded[...])
        fresh = (static[piece].astype(jnp.float32) + mesh_sum).astype(jnp.bfloat16)
        state[0, first // BLOCK : first // BLOCK + HALF] = fresh.reshape(HALF, BLOCK, width)
        if first == 0:
            pl.semaphore_wait(barrier, len(OFFSETS))
            ship(0)

    copies["edge_bias"].wait()
    copies["node_bias"].wait()
    copies["norm_gain"].wait()
    for layer in range(LAYERS):
        copies["layer", layer, 0].wait()
        now = state[layer].reshape(rows, width)
        source[...] = 0.5 * dot(now, w_send[layer]) + 0.5 * edge_bias[layer : layer + 1]
        copies["layer", layer, 1].wait()
        table[:blocks] = (0.5 * dot(now, w_recv[layer])).reshape(blocks, BLOCK, width)
        copies["layer", layer, 2].wait()
        own[...] = 0.5 * dot(now, w_self[layer]) + 0.5 * node_bias[layer : layer + 1]
        for number in range(len(OFFSETS)):
            sends[layer, number].wait_recv()
        theirs = arrived[layer].reshape(-1, width)
        table[blocks:] = (0.5 * dot(theirs, w_recv[layer])).reshape(-1, BLOCK, width)
        copies["layer", layer, 3].wait()
        copies["layer", layer, 4].wait()
        for first in range(0, blocks, HALF):

            def edges(b, carry):
                for chunk in range(0, BLOCK, CHUNK):
                    at = pl.ds(pl.multiple_of(b * BLOCK, BLOCK) + chunk, CHUNK)
                    mine = source[at]
                    total = None
                    for k in range(K):
                        row = where_row[b * K + k]
                        h = mine + table[row, chunk : chunk + CHUNK]
                        edge = silu_of_half(h)
                        total = edge if total is None else total + edge
                    gathered[at] = total.astype(jnp.bfloat16)
                return carry

            lax.fori_loop(first, first + HALF, edges, 0)
            piece = pl.ds(first * BLOCK, half)
            update = silu_of_half(own[piece] + 0.5 * dot(gathered[piece], w_gathered[layer]))
            projected = dot(update.astype(jnp.bfloat16), w_out[layer])
            center = jnp.mean(projected, axis=-1, keepdims=True)
            away = projected - center
            spread = jnp.mean(away * away, axis=-1, keepdims=True)
            normed = away * lax.rsqrt(spread + 1e-05) * norm_gain[layer : layer + 1]
            tiles = slice(first, first + HALF)
            before = state[layer, tiles].reshape(half, width).astype(jnp.float32)
            state[layer + 1, tiles] = (
                (before + normed).astype(jnp.bfloat16).reshape(HALF, BLOCK, width)
            )
            if first == 0 and layer + 1 < LAYERS:
                ship(layer + 1)

    copies["w_decode"].wait()
    table[:blocks] = (0.5 * dot(state[LAYERS].reshape(rows, width), w_decode[...])).reshape(
        blocks, BLOCK, width
    )
    copies["w_final"].wait()
    writes = []
    for first in range(0, grid_rows, half):
        for g in range(first // BLOCK, (first + half) // BLOCK):
            at = pl.ds(g * BLOCK, BLOCK)
            tied = table[grid_links[g]]
            encoded[at] = silu_of_half(tied + 0.5 * encoded[at].astype(jnp.float32)).astype(
                jnp.bfloat16
            )
        piece = pl.ds(first, half)
        out[piece] = dot(encoded[piece], w_final[...])
        write = pltpu.make_async_copy(out.at[piece], out_hbm.at[piece], out_sem.at[first // half])
        write.start()
        writes.append(write)
    for write in writes:
        write.wait()
    for copy in sends.values():
        copy.wait_send()


def local(grid_in, mesh_static, block_links, grid_links, *weights):
    bf16, f32 = jnp.bfloat16, jnp.float32
    n = lax.axis_size("dom")
    rows, width = mesh_static.shape
    blocks = rows // BLOCK
    grid_rows, fields = grid_in.shape
    grid_blocks = grid_rows // BLOCK
    remote = len(OFFSETS) * CAP
    outputs = weights[-1].shape[1]
    scratch = [
        pltpu.VMEM(grid_in.shape, bf16),
        pltpu.VMEM(mesh_static.shape, bf16),
    ]
    scratch += [pltpu.VMEM(w.shape, w.dtype) for w in weights]
    scratch += [
        pltpu.VMEM((grid_rows, width), bf16),
        pltpu.VMEM((LAYERS + 1, blocks, BLOCK, width), bf16),
        pltpu.VMEM((rows, width), f32),
        pltpu.VMEM((rows, width), f32),
        pltpu.VMEM((blocks + remote, BLOCK, width), f32),
        pltpu.VMEM((rows, width), bf16),
        pltpu.VMEM((LAYERS, len(OFFSETS), CAP, BLOCK, width), bf16),
        pltpu.VMEM((LAYERS, len(OFFSETS), CAP, BLOCK, width), bf16),
        pltpu.VMEM((grid_rows, outputs), f32),
        pltpu.SMEM((blocks * K,), jnp.int32),
        pltpu.SemaphoreType.DMA((7,)),
        pltpu.SemaphoreType.DMA((LAYERS, 5)),
        pltpu.SemaphoreType.DMA((grid_rows // (HALF * BLOCK),)),
        pltpu.SemaphoreType.DMA((grid_rows // (HALF * BLOCK),)),
        pltpu.SemaphoreType.DMA((LAYERS, len(OFFSETS))),
        pltpu.SemaphoreType.DMA((LAYERS, len(OFFSETS))),
    ]
    anywhere = pl.BlockSpec(memory_space=pl.ANY)
    return pl.pallas_call(
        functools.partial(kernel, n, blocks, grid_blocks),
        out_shape=jax.ShapeDtypeStruct((grid_rows, outputs), f32),
        in_specs=[pl.BlockSpec(memory_space=pltpu.SMEM)] * 2 + [anywhere] * (2 + len(weights)),
        out_specs=anywhere,
        scratch_shapes=scratch,
        compiler_params=pltpu.CompilerParams(
            collective_id=0, has_side_effects=True, vmem_limit_bytes=56 * 1024 * 1024
        ),
    )(grid_links, block_links.T, grid_in, mesh_static, *weights)


def solution(mesh):
    whole = P()
    split = P(("groups", "dom"), None)
    in_specs = (split, P("dom", None), whole, P("dom")) + (whole,) * 11
    return jax.shard_map(
        local, mesh=mesh, in_specs=in_specs, out_specs=split, check_vma=False
    )
```

time: 71.6 us -> 35.7 us (0.50)
  Pallas kernels: 0 us -> 33.3 us
  matrix products: 21.5 us -> 0 us
  starting transfers between devices: 19.4 us -> 0 us
  other arithmetic: 14.5 us -> 0 us
  local copies, waits for them, and re-layouts: 10.1 us -> 2.26 us
  waiting for transfers between devices: 5.24 us -> 0 us
    pallas_call x0 -> x1, Pallas kernels: none -> 33.3 us  [local(): pl.pallas_call(functools.partial(kernel, n, blocks, grid_blocks), out_sha...]
    dot_general x13 -> x0, matrix products: 21.5 us -> none  [the longest x2 5.11 us: local(): projected = jnp.dot(update, w_out[layer], preferred_element_type=f32)]
    ppermute x8 -> x0, starting transfers between devices: 19.4 us -> none  [shifted(): return lax.ppermute(block, axis, route)]
    reduce_sum x4 -> x0, other arithmetic: 10.3 us -> none  [the longest x2 9.81 us: local(): gathered = jnp.sum(edges, axis=1).reshape(-1, width).astype(jnp.bfloat16)]
    gather x3 -> x0, local copies, waits for them, and re-layouts: 6.14 us -> none  [the longest x2 5.53 us: local(): jnp.take(table, where_row.reshape(-1), axis=0)]
    ppermute x8 -> x0, waiting for transfers between devices: 5.24 us -> none  [shifted(): return lax.ppermute(block, axis, route)]
    concatenate x4 -> x0, other arithmetic: 3.13 us -> none  [the longest x2 1.71 us: local(): jnp.concatenate([own_proj, remote_proj], axis=0).reshape(-1, BLOCK, width)]
    reshape x3 -> x0, local copies, waits for them, and re-layouts: 0.78 us -> none  [the longest x1 0.51 us: local(): encoded.reshape(grid_blocks, BLOCK * width)]
  transfers between devices with their start and end apart: 8 -> 0, of which waited for: 3 -> 0; matrix products, arithmetic and copies ran while one was open for 14% -> 0% of each run, Pallas kernels for 0% -> 0%
where the time goes in v1:
time: 35.7 us; the launch traced here: 35.6 us
  Pallas kernels  33.3 us (93%)
  local copies, waits for them, and re-layouts  2.26 us (6%)
    pallas_call x1, Pallas kernels, local(): pl.pallas_call(functools.partial(kernel, n, blocks, grid_blocks), out_sha...  33.3 us
    unnamed x1, local copies, waits for them, and re-layouts  2.26 us

profile of v1, /device:TPU:0, one launch (start us, length us, event | category | flops | bytes accessed | tf_op | source)
XLA Modules:
  0.0 35.6 jit_solution(6708208333758949724)
XLA Ops:
  0.0 33.3 %shard_map.145 = f32[1024,256]{1,0:T(8,128)} custom-call(s32[16]{0:T(128)} %grid_links.1, s32[4,128]{1,0:T(4,128)} %bitcast.1, bf16[1024,384]{1,0:T(8,128)(2,1)} %grid_hbm.1, bf16[512,512]{1,0:T(8,128)(2,1)} %static_hbm.1, bf16[384,512]{1,0:T(8,128)(2,1)} %refs_0_.1, bf16[2,512,512]{2,1,0:T(8,128)(2,1)} %refs_1_.1, bf16[2,512,512]{2,1,0:T(8,128)(2,1)} %refs_2_.1, ...), custom_call_target="tpu_custom_call" | custom-call | tf_op jit(solution)/shard_map/pallas_call | solution.py:295
  33.3 2.3 %copy.17 = f32[1024,256]{1,0:T(8,128)} copy(f32[1024,256]{1,0:T(8,128)} %shard_map.145) | data formatting | bytes 2097152

commit v2 on v1

v2 whole, which is shorter than its diff:
```python
import functools

import jax
import jax.numpy as jnp
from jax import lax
from jax.experimental import pallas as pl
from jax.experimental.pallas import tpu as pltpu
from jax.sharding import PartitionSpec as P

BLOCK = 64
K = 4
NBD = 3
CAP = 2
LAYERS = 2
OFFSETS = (1, -1, 2, -2)
PARTS = 2
CHUNK = 16
MESH_ID = pl.DeviceIdType.MESH


def dot(a, b):
    return jnp.dot(a, b, preferred_element_type=jnp.float32)


def silu_of_half(h):
    return h + h * jnp.tanh(h)


def span(values, owner, blocks):
    low, high = NBD - 1, 0
    for value in values:
        within = value - owner * blocks
        named = (within >= 0) & (within < blocks)
        low = jnp.where(named, jnp.minimum(low, within), low)
        high = jnp.where(named, jnp.maximum(high, within), high)
    return low, high


def kernel(n, blocks, grid_blocks, grid_links, links, grid_hbm, static_hbm, *refs):
    weights_hbm = refs[:11]
    out_hbm = refs[11]
    weights = refs[12:23]
    (
        grid_in,
        static,
        encoded,
        state,
        source,
        own,
        table,
        gathered,
        stage,
        arrived,
        out,
        where_row,
        w_sem,
        layer_sem,
        grid_sem,
        static_sem,
        out_sem,
        send_sem,
        recv_sem,
    ) = refs[23:]
    (
        w_encode,
        w_send,
        w_recv,
        edge_bias,
        w_self,
        w_gathered,
        node_bias,
        w_out,
        norm_gain,
        w_decode,
        w_final,
    ) = weights
    me = lax.axis_index("dom")
    sides = [lax.rem(me + offset + n, n) for offset in OFFSETS]
    width = state.shape[4]
    nodes = BLOCK // PARTS
    rows = blocks * nodes
    grid_rows = grid_blocks * nodes
    f32, bf16 = jnp.float32, jnp.bfloat16

    barrier = pltpu.get_barrier_semaphore()
    for side in sides:
        pl.semaphore_signal(barrier, inc=1, device_id={"dom": side}, device_id_type=MESH_ID)

    copies = {}

    def fetch(name, src, dst, sem):
        copies[name] = pltpu.make_async_copy(src, dst, sem)
        copies[name].start()

    def fetch_weight(number):
        fetch(number, weights_hbm[number], weights[number], w_sem.at[number])

    fetch_weight(0)
    for part in range(PARTS):
        piece = pl.ds(part * nodes, nodes)
        fetch(("grid", part), grid_hbm.at[:, piece], grid_in.at[part], grid_sem.at[part])
        fetch(("static", part), static_hbm.at[:, piece], static.at[part], static_sem.at[part])
    for number in (3, 6, 8):
        fetch_weight(number)
    for layer in range(LAYERS):
        for number in (1, 2, 4, 5, 7):
            fetch(
                (layer, number),
                weights_hbm[number].at[layer],
                weights[number].at[layer],
                layer_sem.at[layer, number],
            )
    fetch_weight(9)
    fetch_weight(10)

    def rows_of(owner):
        return [links[k, owner * blocks + b] for b in range(blocks) for k in range(K)]

    wanted = [span(rows_of(side), me, blocks) for side in sides]
    named = [span(rows_of(me), side, blocks) for side in sides]
    for b in range(blocks):
        for k in range(K):
            value = links[k, me * blocks + b]
            row = jnp.clip(value - me * blocks, 0, blocks - 1)
            for number, side in enumerate(sides):
                within = value - side * blocks
                theirs = (within >= 0) & (within < blocks)
                slot = jnp.where(within == named[number][0], 0, 1)
                row = jnp.where(theirs, blocks + number * CAP + slot, row)
            where_row[b * K + k] = row

    column = lax.broadcasted_iota(jnp.int32, (8, grid_rows), 1)
    key = jnp.zeros((8, grid_rows), jnp.int32)
    for g in range(grid_blocks):
        key = jnp.where(column // nodes == g, grid_links[g] * nodes - g * nodes, key)
    key = (key + column)[:1]
    line = lax.broadcasted_iota(jnp.int32, (rows, grid_rows), 0)
    spreader = jnp.where(line == key, 1.0, 0.0).astype(bf16)

    sends = {}

    def ship(layer, part):
        for number, side in enumerate(sides):
            for slot in range(CAP):
                stage[layer, part, number, slot] = state[layer, part, wanted[number][slot]]
            send = pltpu.make_async_remote_copy(
                src_ref=stage.at[layer, part, number],
                dst_ref=arrived.at[layer, part, number ^ 1],
                send_sem=send_sem.at[layer, part, number],
                recv_sem=recv_sem.at[layer, part, number ^ 1],
                device_id={"dom": side},
                device_id_type=MESH_ID,
            )
            send.start()
            sends[layer, part, number] = send

    def encode(part):
        copies["grid", part].wait()
        fields = grid_in[part].reshape(grid_rows, -1)
        fresh = silu_of_half(0.5 * dot(fields, w_encode[...])).astype(bf16)
        encoded[part] = fresh.reshape(grid_blocks, nodes, width)
        mesh_sum = dot(spreader, fresh)
        copies["static", part].wait()
        begun = static[part].reshape(rows, width).astype(f32) + mesh_sum
        state[0, part] = begun.astype(bf16).reshape(blocks, nodes, width)

    def project(layer, part):
        now = state[layer, part].reshape(rows, width)
        source[part] = 0.5 * dot(now, w_send[layer]) + 0.5 * edge_bias[layer : layer + 1]
        table[part, :blocks] = (0.5 * dot(now, w_recv[layer])).reshape(blocks, nodes, width)
        own[part] = 0.5 * dot(now, w_self[layer]) + 0.5 * node_bias[layer : layer + 1]

    def process(layer, part):
        for number in range(len(OFFSETS)):
            sends[layer, part, number].wait_recv()
        theirs = arrived[layer, part].reshape(-1, width)
        table[part, blocks:] = (0.5 * dot(theirs, w_recv[layer])).reshape(-1, nodes, width)

        def edges(b, carry):
            for chunk in range(0, nodes, CHUNK):
                at = pl.ds(pl.multiple_of(b * nodes, nodes) + chunk, CHUNK)
                mine = source[part, at]
                total = None
                for k in range(K):
                    edge = silu_of_half(mine + table[part, where_row[b * K + k], chunk : chunk + CHUNK])
                    total = edge if total is None else total + edge
                gathered[part, at] = total.astype(bf16)
            return carry

        lax.fori_loop(0, blocks, edges, 0)
        update = silu_of_half(own[part] + 0.5 * dot(gathered[part], w_gathered[layer]))
        projected = dot(update.astype(bf16), w_out[layer])
        center = jnp.mean(projected, axis=-1, keepdims=True)
        away = projected - center
        spread = jnp.mean(away * away, axis=-1, keepdims=True)
        normed = away * lax.rsqrt(spread + 1e-05) * norm_gain[layer : layer + 1]
        before = state[layer, part].reshape(rows, width).astype(f32)
        state[layer + 1, part] = (before + normed).astype(bf16).reshape(blocks, nodes, width)

    writes = []

    def decode(part):
        last = state[LAYERS, part].reshape(rows, width)
        table[part, :blocks] = (0.5 * dot(last, w_decode[...])).reshape(blocks, nodes, width)
        for g in range(grid_blocks):
            h = table[part, grid_links[g]] + 0.5 * encoded[part, g].astype(f32)
            encoded[part, g] = silu_of_half(h).astype(bf16)
        found = dot(encoded[part].reshape(grid_rows, width), w_final[...])
        out[part] = found.reshape(grid_blocks, nodes, -1)
        write = pltpu.make_async_copy(
            out.at[part], out_hbm.at[:, pl.ds(part * nodes, nodes)], out_sem.at[part]
        )
        write.start()
        writes.append(write)

    copies[0].wait()
    for part in range(PARTS):
        encode(part)
        if part == 0:
            pl.semaphore_wait(barrier, len(OFFSETS))
        ship(0, part)
    for number in (3, 6, 8):
        copies[number].wait()
    for layer in range(LAYERS):
        for number in (1, 2, 4):
            copies[layer, number].wait()
        for part in range(PARTS):
            project(layer, part)
        for number in (5, 7):
            copies[layer, number].wait()
        if layer == LAYERS - 1:
            copies[9].wait()
            copies[10].wait()
        for part in range(PARTS):
            process(layer, part)
            if layer + 1 < LAYERS:
                ship(layer + 1, part)
            else:
                decode(part)
    for write in writes:
        write.wait()
    for send in sends.values():
        send.wait_send()


def local(grid_in, mesh_static, block_links, grid_links, *weights):
    bf16, f32 = jnp.bfloat16, jnp.float32
    n = lax.axis_size("dom")
    rows, width = mesh_static.shape
    blocks = rows // BLOCK
    grid_rows, fields = grid_in.shape
    grid_blocks = grid_rows // BLOCK
    nodes = BLOCK // PARTS
    sides = len(OFFSETS)
    outputs = weights[-1].shape[1]
    scratch = [pltpu.VMEM(w.shape, w.dtype) for w in weights]
    scratch += [
        pltpu.VMEM((PARTS, grid_blocks, nodes, fields), bf16),
        pltpu.VMEM((PARTS, blocks, nodes, width), bf16),
        pltpu.VMEM((PARTS, grid_blocks, nodes, width), bf16),
        pltpu.VMEM((LAYERS + 1, PARTS, blocks, nodes, width), bf16),
        pltpu.VMEM((PARTS, blocks * nodes, width), f32),
        pltpu.VMEM((PARTS, blocks * nodes, width), f32),
        pltpu.VMEM((PARTS, blocks + sides * CAP, nodes, width), f32),
        pltpu.VMEM((PARTS, blocks * nodes, width), bf16),
        pltpu.VMEM((LAYERS, PARTS, sides, CAP, nodes, width), bf16),
        pltpu.VMEM((LAYERS, PARTS, sides, CAP, nodes, width), bf16),
        pltpu.VMEM((PARTS, grid_blocks, nodes, outputs), f32),
        pltpu.SMEM((blocks * K,), jnp.int32),
        pltpu.SemaphoreType.DMA((len(weights),)),
        pltpu.SemaphoreType.DMA((LAYERS, len(weights))),
        pltpu.SemaphoreType.DMA((PARTS,)),
        pltpu.SemaphoreType.DMA((PARTS,)),
        pltpu.SemaphoreType.DMA((PARTS,)),
        pltpu.SemaphoreType.DMA((LAYERS, PARTS, sides)),
        pltpu.SemaphoreType.DMA((LAYERS, PARTS, sides)),
    ]
    anywhere = pl.BlockSpec(memory_space=pl.ANY)
    found = pl.pallas_call(
        functools.partial(kernel, n, blocks, grid_blocks),
        out_shape=jax.ShapeDtypeStruct((grid_blocks, BLOCK, outputs), f32),
        in_specs=[pl.BlockSpec(memory_space=pltpu.SMEM)] * 2 + [anywhere] * (2 + len(weights)),
        out_specs=anywhere,
        scratch_shapes=scratch,
        compiler_params=pltpu.CompilerParams(
            collective_id=0, has_side_effects=True, vmem_limit_bytes=56 * 1024 * 1024
        ),
    )(
        grid_links,
        block_links.T,
        grid_in.reshape(grid_blocks, BLOCK, fields),
        mesh_static.reshape(blocks, BLOCK, width),
        *weights,
    )
    return found.reshape(grid_rows, outputs)


def solution(mesh):
    whole = P()
    split = P(("groups", "dom"), None)
    in_specs = (split, P("dom", None), whole, P("dom")) + (whole,) * 11
    return jax.shard_map(
        local, mesh=mesh, in_specs=in_specs, out_specs=split, check_vma=False
    )
```

time: 35.7 us -> 33.4 us (0.936)
  Pallas kernels: 33.3 us -> 31 us
    pallas_call x1, Pallas kernels: 33.3 us -> 31 us  [local(): pl.pallas_call(functools.partial(kernel, n, blocks, grid_blocks), out_sha...]
where the time goes in v2:
time: 33.4 us; the launch traced here: 33.3 us
  Pallas kernels  31 us (93%)
  local copies, waits for them, and re-layouts  2.26 us (7%)
    pallas_call x1, Pallas kernels, local(): pl.pallas_call(functools.partial(kernel, n, blocks, grid_blocks), out_sha...  31 us
    unnamed x1, local copies, waits for them, and re-layouts  2.26 us

profile of v2, /device:TPU:0, one launch (start us, length us, event | category | flops | bytes accessed | tf_op | source)
XLA Modules:
  0.0 33.3 jit_solution(5861831540441472042)
XLA Ops:
  0.0 31.0 %shard_map.145 = f32[16,64,256]{2,1,0:T(8,128)} custom-call(s32[16]{0:T(128)} %grid_links.1, s32[4,128]{1,0:T(4,128)} %bitcast.7, bf16[16,64,384]{2,1,0:T(8,128)(2,1)} %bitcast.5, bf16[8,64,512]{2,1,0:T(8,128)(2,1)} %bitcast.6, bf16[384,512]{1,0:T(8,128)(2,1)} %refs_0_.1, bf16[2,512,512]{2,1,0:T(8,128)(2,1)} %refs_1_.1, bf16[2,512,512]{2,1,0:T(8,128)(2,1)} %refs_2_.1, ...), custom_call_target="tpu_custom_call" | custom-call | tf_op jit(solution)/shard_map/pallas_call | solution.py:279
  31.0 2.3 %copy.17 = f32[1024,256]{1,0:T(8,128)} copy(f32[1024,256]{1,0:T(8,128)} %bitcast.4) | data formatting | bytes 2097152

commit v3 on v2

--- a/solution.py
+++ b/solution.py
@@ -12,7 +12,9 @@
 NBD = 3
 CAP = 2
 LAYERS = 2
-OFFSETS = (1, -1, 2, -2)
+NEAR, RELAY, PARTNER, FAR = range(4)
+BASE = (0, NBD, 2 * NBD, 2 * NBD + CAP)
+REMOTE = 2 * (NBD + CAP)
 PARTS = 2
 CHUNK = 16
 MESH_ID = pl.DeviceIdType.MESH
@@ -75,7 +77,12 @@
         w_final,
     ) = weights
     me = lax.axis_index("dom")
-    sides = [lax.rem(me + offset + n, n) for offset in OFFSETS]
+    toward = 2 * lax.rem(me, 2) - 1
+    near = lax.rem(me + toward + n, n)
+    behind = lax.rem(me - 2 * toward + n, n)
+    partner = lax.rem(me - toward + n, n)
+    ahead = lax.rem(me + 2 * toward + n, n)
+    sides = (near, behind, partner, ahead)
     width = state.shape[4]
     nodes = BLOCK // PARTS
     rows = blocks * nodes
@@ -116,8 +123,8 @@
     def rows_of(owner):
         return [links[k, owner * blocks + b] for b in range(blocks) for k in range(K)]
 
-    wanted = [span(rows_of(side), me, blocks) for side in sides]
-    named = [span(rows_of(me), side, blocks) for side in sides]
+    wanted = {PARTNER: span(rows_of(partner), me, blocks), FAR: span(rows_of(behind), me, blocks)}
+    named = {number: span(rows_of(me), sides[number], blocks) for number in (PARTNER, FAR)}
     for b in range(blocks):
         for k in range(K):
             value = links[k, me * blocks + b]
@@ -125,8 +132,11 @@
             for number, side in enumerate(sides):
                 within = value - side * blocks
                 theirs = (within >= 0) & (within < blocks)
-                slot = jnp.where(within == named[number][0], 0, 1)
-                row = jnp.where(theirs, blocks + number * CAP + slot, row)
+                if number in named:
+                    slot = jnp.where(within == named[number][0], 0, 1)
+                else:
+                    slot = jnp.clip(within, 0, NBD - 1)
+                row = jnp.where(theirs, blocks + BASE[number] + slot, row)
             where_row[b * K + k] = row
 
     column = lax.broadcasted_iota(jnp.int32, (8, grid_rows), 1)
@@ -139,20 +149,24 @@
 
     sends = {}
 
+    def send(layer, part, number, src, side, count):
+        copy = pltpu.make_async_remote_copy(
+            src_ref=src,
+            dst_ref=arrived.at[layer, part, pl.ds(BASE[number], count)],
+            send_sem=send_sem.at[layer, part, number],
+            recv_sem=recv_sem.at[layer, part, number],
+            device_id={"dom": side},
+            device_id_type=MESH_ID,
+        )
+        copy.start()
+        sends[layer, part, number] = copy
+
     def ship(layer, part):
-        for number, side in enumerate(sides):
+        send(layer, part, NEAR, state.at[layer, part, pl.ds(0, NBD)], near, NBD)
+        for number, side in ((FAR, behind), (PARTNER, partner)):
             for slot in range(CAP):
-                stage[layer, part, number, slot] = state[layer, part, wanted[number][slot]]
-            send = pltpu.make_async_remote_copy(
-                src_ref=stage.at[layer, part, number],
-                dst_ref=arrived.at[layer, part, number ^ 1],
-                send_sem=send_sem.at[layer, part, number],
-                recv_sem=recv_sem.at[layer, part, number ^ 1],
-                device_id={"dom": side},
-                device_id_type=MESH_ID,
-            )
-            send.start()
-            sends[layer, part, number] = send
+                stage[layer, part, number - PARTNER, slot] = state[layer, part, wanted[number][slot]]
+            send(layer, part, number, stage.at[layer, part, number - PARTNER], side, CAP)
 
     def encode(part):
         copies["grid", part].wait()
@@ -171,7 +185,10 @@
         own[part] = 0.5 * dot(now, w_self[layer]) + 0.5 * node_bias[layer : layer + 1]
 
     def process(layer, part):
-        for number in range(len(OFFSETS)):
+        sends[layer, part, NEAR].wait_recv()
+        passed = arrived.at[layer, part, pl.ds(BASE[NEAR], NBD)]
+        send(layer, part, RELAY, passed, partner, NBD)
+        for number in (PARTNER, FAR, RELAY):
             sends[layer, part, number].wait_recv()
         theirs = arrived[layer, part].reshape(-1, width)
         table[part, blocks:] = (0.5 * dot(theirs, w_recv[layer])).reshape(-1, nodes, width)
@@ -217,7 +234,7 @@
     for part in range(PARTS):
         encode(part)
         if part == 0:
-            pl.semaphore_wait(barrier, len(OFFSETS))
+            pl.semaphore_wait(barrier, len(sides))
         ship(0, part)
     for number in (3, 6, 8):
         copies[number].wait()
@@ -239,8 +256,8 @@
                 decode(part)
     for write in writes:
         write.wait()
-    for send in sends.values():
-        send.wait_send()
+    for copy in sends.values():
+        copy.wait_send()
 
 
 def local(grid_in, mesh_static, block_links, grid_links, *weights):
@@ -251,7 +268,6 @@
     grid_rows, fields = grid_in.shape
     grid_blocks = grid_rows // BLOCK
     nodes = BLOCK // PARTS
-    sides = len(OFFSETS)
     outputs = weights[-1].shape[1]
     scratch = [pltpu.VMEM(w.shape, w.dtype) for w in weights]
     scratch += [
@@ -261,10 +277,10 @@
         pltpu.VMEM((LAYERS + 1, PARTS, blocks, nodes, width), bf16),
         pltpu.VMEM((PARTS, blocks * nodes, width), f32),
         pltpu.VMEM((PARTS, blocks * nodes, width), f32),
-        pltpu.VMEM((PARTS, blocks + sides * CAP, nodes, width), f32),
+        pltpu.VMEM((PARTS, blocks + REMOTE, nodes, width), f32),
         pltpu.VMEM((PARTS, blocks * nodes, width), bf16),
-        pltpu.VMEM((LAYERS, PARTS, sides, CAP, nodes, width), bf16),
-        pltpu.VMEM((LAYERS, PARTS, sides, CAP, nodes, width), bf16),
+        pltpu.VMEM((LAYERS, PARTS, 2, CAP, nodes, width), bf16),
+        pltpu.VMEM((LAYERS, PARTS, REMOTE, nodes, width), bf16),
         pltpu.VMEM((PARTS, grid_blocks, nodes, outputs), f32),
         pltpu.SMEM((blocks * K,), jnp.int32),
         pltpu.SemaphoreType.DMA((len(weights),)),
@@ -272,8 +288,8 @@
         pltpu.SemaphoreType.DMA((PARTS,)),
         pltpu.SemaphoreType.DMA((PARTS,)),
         pltpu.SemaphoreType.DMA((PARTS,)),
-        pltpu.SemaphoreType.DMA((LAYERS, PARTS, sides)),
-        pltpu.SemaphoreType.DMA((LAYERS, PARTS, sides)),
+        pltpu.SemaphoreType.DMA((LAYERS, PARTS, 4)),
+        pltpu.SemaphoreType.DMA((LAYERS, PARTS, 4)),
     ]
     anywhere = pl.BlockSpec(memory_space=pl.ANY)
     found = pl.pallas_call(

time: 33.4 us -> 32.8 us (0.982)
  Pallas kernels: 31 us -> 30.3 us
    pallas_call x1, Pallas kernels: 31 us -> 30.3 us  [local(): pl.pallas_call(functools.partial(kernel, n, blocks, grid_blocks), out_sha...]
where the time goes in v3:
time: 32.8 us; the launch traced here: 32.6 us
  Pallas kernels  30.3 us (92%)
  local copies, waits for them, and re-layouts  2.26 us (7%)
    pallas_call x1, Pallas kernels, local(): pl.pallas_call(functools.partial(kernel, n, blocks, grid_blocks), out_sha...  30.3 us
    unnamed x1, local copies, waits for them, and re-layouts  2.26 us

profile of v3, /device:TPU:0, one launch (start us, length us, event | category | flops | bytes accessed | tf_op | source)
XLA Modules:
  0.0 32.6 jit_solution(4165413255782701682)
XLA Ops:
  0.0 30.3 %shard_map.145 = f32[16,64,256]{2,1,0:T(8,128)} custom-call(s32[16]{0:T(128)} %grid_links.1, s32[4,128]{1,0:T(4,128)} %bitcast.7, bf16[16,64,384]{2,1,0:T(8,128)(2,1)} %bitcast.5, bf16[8,64,512]{2,1,0:T(8,128)(2,1)} %bitcast.6, bf16[384,512]{1,0:T(8,128)(2,1)} %refs_0_.1, bf16[2,512,512]{2,1,0:T(8,128)(2,1)} %refs_1_.1, bf16[2,512,512]{2,1,0:T(8,128)(2,1)} %refs_2_.1, ...), custom_call_target="tpu_custom_call" | custom-call | tf_op jit(solution)/shard_map/pallas_call | solution.py:295
  30.3 2.3 %copy.17 = f32[1024,256]{1,0:T(8,128)} copy(f32[1024,256]{1,0:T(8,128)} %bitcast.4) | data formatting | bytes 2097152

commit v4 on v3

--- a/solution.py
+++ b/solution.py
@@ -292,14 +292,15 @@
         pltpu.SemaphoreType.DMA((LAYERS, PARTS, 4)),
     ]
     anywhere = pl.BlockSpec(memory_space=pl.ANY)
+    in_hbm = pl.BlockSpec(memory_space=pltpu.HBM)
     found = pl.pallas_call(
         functools.partial(kernel, n, blocks, grid_blocks),
         out_shape=jax.ShapeDtypeStruct((grid_blocks, BLOCK, outputs), f32),
-        in_specs=[pl.BlockSpec(memory_space=pltpu.SMEM)] * 2 + [anywhere] * (2 + len(weights)),
+        in_specs=[pl.BlockSpec(memory_space=pltpu.SMEM)] * 2 + [in_hbm] * (2 + len(weights)),
         out_specs=anywhere,
         scratch_shapes=scratch,
         compiler_params=pltpu.CompilerParams(
-            collective_id=0, has_side_effects=True, vmem_limit_bytes=56 * 1024 * 1024
+            collective_id=0, has_side_effects=True, vmem_limit_bytes=24 * 1024 * 1024
         ),
     )(
         grid_links,

time: 32.8 us -> 43 us (1.31); the launches traced: 32.6 us -> 42.2 us
  local copies, waits for them, and re-layouts: 2.26 us -> 15 us
  Pallas kernels: 30.3 us -> 27.2 us
    unnamed x1 -> x31, local copies, waits for them, and re-layouts: 2.26 us -> 15 us
    pallas_call x1, Pallas kernels: 30.3 us -> 27.2 us  [local(): pl.pallas_call(functools.partial(kernel, n, blocks, grid_blocks), out_sha...]
where the time goes in v4:
time: 43 us; the launch traced here: 42.2 us
  Pallas kernels  27.2 us (63%)
  local copies, waits for them, and re-layouts  15 us (35%)
    pallas_call x1, Pallas kernels, local(): pl.pallas_call(functools.partial(kernel, n, blocks, grid_blocks), out_sha...  27.2 us
    unnamed x31, local copies, waits for them, and re-layouts  15 us

profile of v4, /device:TPU:0, one launch (start us, length us, event | category | flops | bytes accessed | tf_op | source)
XLA Modules:
  0.0 42.2 jit_solution(13066246274524706602)
XLA Ops:
  0.0 0.0 copy-start.10
  0.0 0.0 copy-start.14
  0.0 0.7 %copy-done.10 = f32[2,512]{1,0:T(2,128)S(1)} copy-done((f32[2,512]{1,0:T(2,128)S(1)}, f32[2,512]{1,0:T(2,128)}, u32[]{:S(2)}) %copy-start.10) | copy-done | bytes 4120
  0.7 0.0 copy-done.14
  0.7 0.0 copy-start
  0.7 1.2 %copy-done = bf16[2,512,512]{2,1,0:T(8,128)(2,1)S(1)} copy-done((bf16[2,512,512]{2,1,0:T(8,128)(2,1)S(1)}, bf16[2,512,512]{2,1,0:T(8,128)(2,1)}, u32[]{:S(2)}) %copy-start) | copy-done | bytes 1048600
  1.9 0.0 copy-start.1
  1.9 1.2 %copy-done.1 = bf16[2,512,512]{2,1,0:T(8,128)(2,1)S(1)} copy-done((bf16[2,512,512]{2,1,0:T(8,128)(2,1)S(1)}, bf16[2,512,512]{2,1,0:T(8,128)(2,1)}, u32[]{:S(2)}) %copy-start.1) | copy-done | bytes 1048600
  3.1 0.0 copy-start.2
  3.1 1.2 %copy-done.2 = bf16[2,512,512]{2,1,0:T(8,128)(2,1)S(1)} copy-done((bf16[2,512,512]{2,1,0:T(8,128)(2,1)S(1)}, bf16[2,512,512]{2,1,0:T(8,128)(2,1)}, u32[]{:S(2)}) %copy-start.2) | copy-done | bytes 1048600
  4.4 0.0 copy-start.3
  4.4 1.2 %copy-done.3 = bf16[2,512,512]{2,1,0:T(8,128)(2,1)S(1)} copy-done((bf16[2,512,512]{2,1,0:T(8,128)(2,1)S(1)}, bf16[2,512,512]{2,1,0:T(8,128)(2,1)}, u32[]{:S(2)}) %copy-start.3) | copy-done | bytes 1048600
  5.6 0.0 copy-start.4
  5.6 1.2 %copy-done.4 = bf16[2,512,512]{2,1,0:T(8,128)(2,1)S(1)} copy-done((bf16[2,512,512]{2,1,0:T(8,128)(2,1)S(1)}, bf16[2,512,512]{2,1,0:T(8,128)(2,1)}, u32[]{:S(2)}) %copy-start.4) | copy-done | bytes 1048600
  6.8 0.0 copy-start.5
  6.8 1.1 %copy-done.5 = bf16[1024,384]{1,0:T(8,128)(2,1)S(1)} copy-done((bf16[1024,384]{1,0:T(8,128)(2,1)S(1)}, bf16[1024,384]{1,0:T(8,128)(2,1)}, u32[]{:S(2)}) %copy-start.5) | copy-done | bytes 786456
  8.0 0.0 copy-start.6
  8.0 1.0 %copy-done.6 = bf16[512,512]{1,0:T(8,128)(2,1)S(1)} copy-done((bf16[512,512]{1,0:T(8,128)(2,1)S(1)}, bf16[512,512]{1,0:T(8,128)(2,1)}, u32[]{:S(2)}) %copy-start.6) | copy-done | bytes 524312
  9.0 0.0 copy-start.7
  9.0 1.0 %copy-done.7 = bf16[512,512]{1,0:T(8,128)(2,1)S(1)} copy-done((bf16[512,512]{1,0:T(8,128)(2,1)S(1)}, bf16[512,512]{1,0:T(8,128)(2,1)}, u32[]{:S(2)}) %copy-start.7) | copy-done | bytes 524312
  10.0 0.0 copy-start.8
  10.0 1.0 %copy-done.8 = bf16[384,512]{1,0:T(8,128)(2,1)S(1)} copy-done((bf16[384,512]{1,0:T(8,128)(2,1)S(1)}, bf16[384,512]{1,0:T(8,128)(2,1)}, u32[]{:S(2)}) %copy-start.8) | copy-done | bytes 393240
  11.0 0.0 copy-start.9
  11.0 0.9 %copy-done.9 = bf16[512,256]{1,0:T(8,128)(2,1)S(1)} copy-done((bf16[512,256]{1,0:T(8,128)(2,1)S(1)}, bf16[512,256]{1,0:T(8,128)(2,1)}, u32[]{:S(2)}) %copy-start.9) | copy-done | bytes 262168
  12.0 0.0 copy-start.11
  12.0 0.7 %copy-done.11 = f32[2,512]{1,0:T(2,128)S(1)} copy-done((f32[2,512]{1,0:T(2,128)S(1)}, f32[2,512]{1,0:T(2,128)}, u32[]{:S(2)}) %copy-start.11) | copy-done | bytes 4120
  12.7 0.0 copy-start.12
  12.7 0.7 %copy-done.12 = f32[2,512]{1,0:T(2,128)S(1)} copy-done((f32[2,512]{1,0:T(2,128)S(1)}, f32[2,512]{1,0:T(2,128)}, u32[]{:S(2)}) %copy-start.12) | copy-done | bytes 4120
  13.4 0.0 copy-start.13
  13.4 0.7 %copy-done.13 = s32[128,4]{0,1:T(4,128)S(1)} copy-done((s32[128,4]{0,1:T(4,128)S(1)}, s32[128,4]{0,1:T(4,128)}, u32[]{:S(2)}) %copy-start.13) | copy-done | bytes 2072
  14.0 27.2 %shard_map.145 = f32[16,64,256]{2,1,0:T(8,128)S(1)} custom-call(s32[16]{0:T(128)S(1)} %copy-done.14, s32[4,128]{1,0:T(4,128)S(1)} %bitcast.7, bf16[16,64,384]{2,1,0:T(8,128)(2,1)S(1)} %bitcast.5, bf16[8,64,512]{2,1,0:T(8,128)(2,1)S(1)} %bitcast.6, bf16[384,512]{1,0:T(8,128)(2,1)S(1)} %copy-done.8, bf16[2,512,512]{2,1,0:T(8,128)(2,1)S(1)} %copy-done, ...), custom_call_target="tpu_custom_call" | custom-call | tf_op jit(solution)/shard_map/pallas_call | solution.py:296
  41.2 1.0 %copy.17 = f32[1024,256]{1,0:T(8,128)} copy(f32[1024,256]{1,0:T(8,128)S(1)} %bitcast.4) | data formatting | bytes 2097152
Async XLA Ops:
  0.0 0.7 %copy-start.10 = (f32[2,512]{1,0:T(2,128)S(1)}, f32[2,512]{1,0:T(2,128)}, u32[]{:S(2)}) copy-start(f32[2,512]{1,0:T(2,128)} %refs_3_.1) | copy-start | bytes 12292
  0.0 0.7 %copy-start.14 = (s32[16]{0:T(128)S(1)}, s32[16]{0:T(128)}, u32[]{:S(2)}) copy-start(s32[16]{0:T(128)} %grid_links.1) | copy-start | bytes 196
  0.7 1.2 %copy-start = (bf16[2,512,512]{2,1,0:T(8,128)(2,1)S(1)}, bf16[2,512,512]{2,1,0:T(8,128)(2,1)}, u32[]{:S(2)}) copy-start(bf16[2,512,512]{2,1,0:T(8,128)(2,1)} %refs_1_.1) | copy-start | bytes 3145732
  1.9 1.2 %copy-start.1 = (bf16[2,512,512]{2,1,0:T(8,128)(2,1)S(1)}, bf16[2,512,512]{2,1,0:T(8,128)(2,1)}, u32[]{:S(2)}) copy-start(bf16[2,512,512]{2,1,0:T(8,128)(2,1)} %refs_2_.1) | copy-start | bytes 3145732
  3.1 1.2 %copy-start.2 = (bf16[2,512,512]{2,1,0:T(8,128)(2,1)S(1)}, bf16[2,512,512]{2,1,0:T(8,128)(2,1)}, u32[]{:S(2)}) copy-start(bf16[2,512,512]{2,1,0:T(8,128)(2,1)} %refs_4_.1) | copy-start | bytes 3145732
  4.4 1.2 %copy-start.3 = (bf16[2,512,512]{2,1,0:T(8,128)(2,1)S(1)}, bf16[2,512,512]{2,1,0:T(8,128)(2,1)}, u32[]{:S(2)}) copy-start(bf16[2,512,512]{2,1,0:T(8,128)(2,1)} %refs_5_.1) | copy-start | bytes 3145732
  5.6 1.2 %copy-start.4 = (bf16[2,512,512]{2,1,0:T(8,128)(2,1)S(1)}, bf16[2,512,512]{2,1,0:T(8,128)(2,1)}, u32[]{:S(2)}) copy-start(bf16[2,512,512]{2,1,0:T(8,128)(2,1)} %refs_7_.1) | copy-start | bytes 3145732
  6.8 1.1 %copy-start.5 = (bf16[1024,384]{1,0:T(8,128)(2,1)S(1)}, bf16[1024,384]{1,0:T(8,128)(2,1)}, u32[]{:S(2)}) copy-start(bf16[1024,384]{1,0:T(8,128)(2,1)} %param.15) | copy-start | bytes 2359300
  8.0 1.0 %copy-start.6 = (bf16[512,512]{1,0:T(8,128)(2,1)S(1)}, bf16[512,512]{1,0:T(8,128)(2,1)}, u32[]{:S(2)}) copy-start(bf16[512,512]{1,0:T(8,128)(2,1)} %param.16) | copy-start | bytes 1572868
  9.0 1.0 %copy-start.7 = (bf16[512,512]{1,0:T(8,128)(2,1)S(1)}, bf16[512,512]{1,0:T(8,128)(2,1)}, u32[]{:S(2)}) copy-start(bf16[512,512]{1,0:T(8,128)(2,1)} %refs_9_.1) | copy-start | bytes 1572868
  10.0 1.0 %copy-start.8 = (bf16[384,512]{1,0:T(8,128)(2,1)S(1)}, bf16[384,512]{1,0:T(8,128)(2,1)}, u32[]{:S(2)}) copy-start(bf16[384,512]{1,0:T(8,128)(2,1)} %refs_0_.1) | copy-start | bytes 1179652
  11.0 0.9 %copy-start.9 = (bf16[512,256]{1,0:T(8,128)(2,1)S(1)}, bf16[512,256]{1,0:T(8,128)(2,1)}, u32[]{:S(2)}) copy-start(bf16[512,256]{1,0:T(8,128)(2,1)} %refs_10_.1) | copy-start | bytes 786436
  12.0 0.7 %copy-start.11 = (f32[2,512]{1,0:T(2,128)S(1)}, f32[2,512]{1,0:T(2,128)}, u32[]{:S(2)}) copy-start(f32[2,512]{1,0:T(2,128)} %refs_6_.1) | copy-start | bytes 12292
  12.7 0.7 %copy-start.12 = (f32[2,512]{1,0:T(2,128)S(1)}, f32[2,512]{1,0:T(2,128)}, u32[]{:S(2)}) copy-start(f32[2,512]{1,0:T(2,128)} %refs_8_.1) | copy-start | bytes 12292
  13.4 0.7 %copy-start.13 = (s32[128,4]{0,1:T(4,128)S(1)}, s32[128,4]{0,1:T(4,128)}, u32[]{:S(2)}) copy-start(s32[128,4]{0,1:T(4,128)} %param.17) | copy-start | bytes 6148
